TPU v7x, 512 devices: a whole 4x8x8 slice. The times are simulated.
512 devices in a mesh: ctx: 64 (over y_lo, z, x), tp: 8 (over y_hi, core).
Axes of the slice: x: 4, y: 8 (y_hi: 4, y_lo: 2; y = y_hi * 2 + y_lo), z: 8, core: 2. Of those that a mesh axis runs over, the one named last changes fastest.
Arguments:
- queries: bfloat16 [16384, 8192], P('ctx', 'tp'), may hold values from -128 to 128
- cotangent: bfloat16 [16384, 8192], P('ctx', 'tp'), may hold values from -96 to 96
- image_keys: bfloat16 [64, 64, 1024], P('ctx', None, 'tp'), may hold values from -8 to 8
- image_values: bfloat16 [64, 64, 1024], P('ctx', None, 'tp'), may hold values from -6 to 6
- attn_gate: float32 [1], replicated, may hold values from 0.4 to 1.5
- block_mask: int32 [128, 64], P('ctx'), may hold values from 0 to 1, as said below
- image_owner: int32 [64], replicated, may hold values from 0 to 63, each once
Outputs:
- query_grad: bfloat16 [16384, 8192], P('ctx', 'tp')
- key_grad: bfloat16 [64, 64, 1024], P('ctx', None, 'tp')
- value_grad: bfloat16 [64, 64, 1024], P('ctx', None, 'tp')
- gate_grad: float32 [1], replicated
Inputs may be any that keep to these rules, and one draw needn't show every extreme that they name: `block_mask`: every text block reads at least one image; the 2 blocks of one index of ctx together read exactly 32 distinct images.
All inputs are finite; a program needn't handle non-finite values.
Results may differ from a plain program's by a relative error of at most 0.02.
Values may be sent and summed in bfloat16 or wider, within the bound.
A program may use at most 64 MiB of HBM per device.

v0:
```python
import math

import jax
import jax.numpy as jnp
from jax import lax
from jax.sharding import PartitionSpec as P

HD = 128
BLK = 128


def per_device(queries, cotangent, image_keys, image_values, attn_gate, block_mask, image_owner):
    tok_dev = queries.shape[0]
    local_kv = image_keys.shape[2] // HD
    local_heads = queries.shape[1] // HD
    groups = local_heads // local_kv
    img_tok = image_keys.shape[1]
    inv_root = 1.0 / math.sqrt(HD)
    read_most = lax.axis_size("ctx") // 2
    gathered_keys, gathered_values = (
        lax.all_gather(image_keys, "ctx", axis=0, tiled=True),
        lax.all_gather(image_values, "ctx", axis=0, tiled=True),
    )
    n_images = gathered_keys.shape[0]
    read_any = jnp.max(block_mask, axis=0)
    ranking = read_any * (2 * n_images) + (n_images - 1 - jnp.arange(n_images, dtype=jnp.int32))
    top_vals, image_ids = lax.top_k(ranking, read_most)
    is_read = read_any[image_ids] > 0
    slot_ids = image_owner[image_ids]
    block_keep = (block_mask[:, image_ids] > 0) & is_read[None, :]
    keep_mask = jnp.repeat(jnp.repeat(block_keep, BLK, axis=0), img_tok, axis=1)
    key_rows = jnp.take(gathered_keys, slot_ids, axis=0).reshape(read_most * img_tok, local_kv, HD)
    value_rows = jnp.take(gathered_values, slot_ids, axis=0).reshape(
        read_most * img_tok, local_kv, HD
    )
    query_heads = queries.reshape(tok_dev, local_kv, groups, HD).transpose(2, 0, 1, 3)
    cot_heads = cotangent.reshape(tok_dev, local_kv, groups, HD).transpose(2, 0, 1, 3)
    gate_value = jnp.tanh(attn_gate[0])

    def head_step(state_in, head_inputs):
        key_acc, value_acc, gate_acc = state_in
        query_one, cot_one = head_inputs
        scores = (
            jnp.einsum("tkd,skd->kts", query_one, key_rows, preferred_element_type=jnp.float32)
            * inv_root
        )
        scores = jnp.where(keep_mask, scores, -1e30)
        row_max = jnp.max(scores, axis=-1, keepdims=True)
        exp_terms = jnp.where(keep_mask, jnp.exp(scores - row_max), 0.0)
        prob_full = exp_terms / jnp.sum(exp_terms, axis=-1, keepdims=True)
        prob_half = prob_full.astype(jnp.bfloat16)
        attended = jnp.einsum(
            "kts,skd->tkd", prob_half, value_rows, preferred_element_type=jnp.float32
        )
        cot_f = cot_one.astype(jnp.float32)
        gate_part = jnp.sum(cot_f * attended)
        attn_grad = (gate_value * cot_f).astype(jnp.bfloat16)
        prob_grad = jnp.einsum(
            "tkd,skd->kts", attn_grad, value_rows, preferred_element_type=jnp.float32
        )
        row_delta = jnp.sum(attn_grad.astype(jnp.float32) * attended, axis=-1).T
        score_grad = (prob_full * (prob_grad - row_delta[:, :, None]) * inv_root).astype(
            jnp.bfloat16
        )
        query_grad = jnp.einsum(
            "kts,skd->tkd", score_grad, key_rows, preferred_element_type=jnp.float32
        ).astype(jnp.bfloat16)
        key_acc = key_acc + jnp.einsum(
            "kts,tkd->skd", score_grad, query_one, preferred_element_type=jnp.float32
        )
        value_acc = value_acc + jnp.einsum(
            "kts,tkd->skd", prob_half, attn_grad, preferred_element_type=jnp.float32
        )
        return ((key_acc, value_acc, gate_acc + gate_part), query_grad)

    zero_grads = jnp.zeros((read_most * img_tok, local_kv, HD), jnp.float32)
    init_state = (zero_grads, zero_grads, jnp.zeros((), jnp.float32))
    (key_acc, value_acc, gate_acc), head_grads = lax.scan(
        head_step, init_state, (query_heads, cot_heads)
    )
    query_grad = head_grads.transpose(1, 2, 0, 3).reshape(tok_dev, local_heads * HD)
    stacked = jnp.concatenate(
        [
            key_acc.reshape(read_most, img_tok, local_kv * HD),
            value_acc.reshape(read_most, img_tok, local_kv * HD),
        ],
        axis=-1,
    )
    stacked = jnp.where(is_read[:, None, None], stacked, 0.0)
    buffer = (
        jnp.zeros((n_images, img_tok, 2 * local_kv * HD), jnp.float32).at[slot_ids].add(stacked)
    )
    received = lax.all_to_all(buffer, "ctx", split_axis=0, concat_axis=0, tiled=True)
    summed = jnp.sum(received, axis=0, keepdims=True)
    key_grad = summed[:, :, : local_kv * HD].astype(jnp.bfloat16)
    value_grad = summed[:, :, local_kv * HD :].astype(jnp.bfloat16)
    gate_total = lax.psum(gate_acc, ("ctx", "tp"))
    term_count = tok_dev * lax.axis_size("ctx") * local_heads * lax.axis_size("tp") * HD
    gate_grad = ((1.0 - gate_value * gate_value) * gate_total / math.sqrt(term_count)).reshape(1)
    return (query_grad, key_grad, value_grad, gate_grad)


def solution(mesh):
    in_specs = (
        P("ctx", "tp"),
        P("ctx", "tp"),
        P("ctx", None, "tp"),
        P("ctx", None, "tp"),
        P(),
        P("ctx", None),
        P(),
    )
    out_specs = (P("ctx", "tp"), P("ctx", None, "tp"), P("ctx", None, "tp"), P())
    return jax.shard_map(
        per_device, mesh=mesh, in_specs=in_specs, out_specs=out_specs, check_vma=False
    )
```

profile of v0, /device:TPU:1, one launch (start us, length us, event | category | flops | bytes accessed | tf_op | source)
XLA Modules:
  0.0 885.5 jit_solution(12151461978923027463)
XLA Ops:
  10.9 2.0 top_k.11
  15.1 1.2 copy.35
  16.4 1.0 copy.36
  17.4 253.3 %all-gather.5.cloned.1.call-done = bf16[64,64,128]{2,1,0:T(8,128)(2,1)} async-done(((bf16[1,64,128]{2,1,0:T(8,128)(2,1)}), bf16[64,64,128]{2,1,0:T(8,128)(2,1)}) %all-gather.5.cloned.1.call-update) | async-done | bytes 1048592 | tf_op jit(solution)/shard_map/all_gather | solution.py:22
  270.7 1.9 gather_fusion.4
  272.6 297.7 %all-gather.3.cloned.1.call-done = bf16[64,64,128]{2,1,0:T(8,128)(2,1)} async-done(((bf16[1,64,128]{2,1,0:T(8,128)(2,1)}), bf16[64,64,128]{2,1,0:T(8,128)(2,1)}) %all-gather.3.cloned.1.call-update) | async-done | bytes 1048592 | tf_op jit(solution)/shard_map/all_gather | solution.py:21
  570.4 1.9 gather_fusion.3
  572.4 92.9 %while.17 = (s32[]{:T(128)}, f32[2048,1,128]{0,2,1:T(8,128)}, f32[2048,1,128]{0,2,1:T(8,128)}, f32[]{:T(128)}, bf16[8,256,1,128]{3,1,2,0:T(8,128)(2,1)}, /*index...) while((s32[]{:T(128)}, f32[2048,1,128]{0,2,1:T(8,128)}, ...), condition=%wide.region_7.9_spmd.clone, body=%wide.region_2.8_spmd.clone.sunk | while | flops 814710016 | bytes 48644448 | solution.py:78
  575.2 1.9 fusion.68
  577.8 1.4 fusion.69
  579.3 1.4 fusion.71
  580.7 1.1 fusion.72
  581.8 1.3 fusion.70
  583.1 1.0 copy-done.5
  586.8 1.9 fusion.68
  589.4 1.4 fusion.69
  590.9 1.4 fusion.71
  592.3 1.1 fusion.72
  593.4 1.3 fusion.70
  594.7 1.0 copy-done.5
  598.4 1.9 fusion.68
  601.0 1.4 fusion.69
  602.5 1.4 fusion.71
  603.9 1.1 fusion.72
  605.0 1.3 fusion.70
  606.3 1.0 copy-done.5
  610.1 1.9 fusion.68
  612.7 1.4 fusion.69
  614.1 1.4 fusion.71
  615.5 1.1 fusion.72
  616.6 1.3 fusion.70
  617.9 1.0 copy-done.5
  621.7 1.9 fusion.68
  624.3 1.4 fusion.69
  625.7 1.4 fusion.71
  627.1 1.1 fusion.72
  628.2 1.3 fusion.70
  629.5 1.0 copy-done.5
  633.3 1.9 fusion.68
  635.9 1.4 fusion.69
  637.3 1.4 fusion.71
  638.8 1.1 fusion.72
  639.8 1.3 fusion.70
  641.1 1.0 copy-done.5
  644.9 1.9 fusion.68
  647.5 1.4 fusion.69
  649.0 1.4 fusion.71
  650.4 1.1 fusion.72
  651.4 1.3 fusion.70
  652.7 1.0 copy-done.5
  656.5 1.9 fusion.68
  659.1 1.4 fusion.69
  660.6 1.4 fusion.71
  662.0 1.1 fusion.72
  663.1 1.3 fusion.70
  664.4 1.0 copy-done.5
  665.3 1.6 copy.40
  667.0 1.3 copy.41
  668.3 1.4 maximum_select_fusion
  669.8 2.5 broadcast_in_dim.68
  672.2 6.2 scatter_fusion
  678.5 7.4 all-to-all-start
  685.9 186.7 %psum.7 = f32[]{:T(128)} all-reduce(f32[]{:T(128)} %get-tuple-element.72), channel_id=1, replica_groups=mesh['ctx'=64,'tp'=8] {'ctx','tp'}, use_global_device_ids=true, to_apply=%region_10.12 | all-reduce | flops 1 | bytes 8 | tf_op jit(solution)/shard_map/psum | solution.py:97
  874.5 2.4 reduce_sum.36
  (165 shorter events, 29.4 us)
Async XLA Ops:
  7.2 6.5 copy-start
  7.2 9.2 %copy-start.8 = (bf16[256,1024]{1,0:T(8,128)(2,1)S(1)}, bf16[256,1024]{1,0:T(8,128)(2,1)}, u32[]{:S(2)}) copy-start(bf16[256,1024]{1,0:T(8,128)(2,1)} %param.12) | copy-start | bytes 1572868
  7.2 263.5 %all-gather.5.cloned.1.call-start = ((), (), s32[]{:S(2)}) async-start(), calls=%async_computation.2 | async-start | bytes 1064960 | tf_op jit(solution)/shard_map/all_gather | solution.py:22
  7.9 562.4 %all-gather.3.cloned.1.call-start = ((), (), s32[]{:S(2)}) async-start(), calls=%async_computation.1 | async-start | bytes 1064960 | tf_op jit(solution)/shard_map/all_gather | solution.py:21
  572.4 1.4 copy-start.6
  577.8 1.5 copy-start.1
  579.3 2.5 copy-start.4
  580.7 2.4 copy-start.2
  580.7 3.4 copy-start.7
  583.1 1.0 copy-start.5
  584.0 1.4 copy-start.6
  589.4 1.5 copy-start.1
  590.9 2.5 copy-start.4
  592.3 2.4 copy-start.2
  592.3 3.4 copy-start.7
  594.7 1.0 copy-start.5
  595.7 1.4 copy-start.6
  601.0 1.5 copy-start.1
  602.5 2.5 copy-start.4
  603.9 2.4 copy-start.2
  603.9 3.4 copy-start.7
  606.3 1.0 copy-start.5
  607.3 1.4 copy-start.6
  612.6 1.5 copy-start.1
  614.1 2.5 copy-start.4
  615.5 2.4 copy-start.2
  615.5 3.4 copy-start.7
  617.9 1.0 copy-start.5
  618.9 1.4 copy-start.6
  624.3 1.5 copy-start.1
  625.7 2.5 copy-start.4
  627.1 2.4 copy-start.2
  627.1 3.4 copy-start.7
  629.5 1.0 copy-start.5
  630.5 1.4 copy-start.6
  635.9 1.5 copy-start.1
  637.3 2.5 copy-start.4
  638.7 2.4 copy-start.2
  638.7 3.4 copy-start.7
  641.1 1.0 copy-start.5
  642.1 1.4 copy-start.6
  647.5 1.5 copy-start.1
  649.0 2.5 copy-start.4
  650.3 2.4 copy-start.2
  650.4 3.4 copy-start.7
  652.7 1.0 copy-start.5
  653.7 1.4 copy-start.6
  659.1 1.5 copy-start.1
  660.6 2.5 copy-start.4
  662.0 2.4 copy-start.2
  662.0 3.4 copy-start.7
  664.3 1.0 copy-start.5
  665.3 1.6 copy-start.3
  678.5 194.1 %copy-start.9 = (bf16[8,256,1,128]{3,1,2,0:T(8,128)(2,1)S(1)}, bf16[8,256,1,128]{3,1,2,0:T(8,128)(2,1)}, u32[]{:S(2)}) copy-start(bf16[8,256,1,128]{3,1,2,0:T(8,128)(2,1)} %get-tuple-element.69) | copy-start | bytes 1572868
  678.5 196.0 %all-to-all-start = ((f32[64,64,256]{2,1,0:T(8,128)}), f32[64,64,256]{2,1,0:T(8,128)}, u32[]{:S(2)}, u32[]{:S(2)}) async-start(f32[64,64,256]{2,1,0:T(8,128)} %scatter_fusion), calls=%async_computation | async-start | bytes 8388608 | tf_op jit(solution)/shard_map/all_to_all | solution.py:93
Sparse Core Ops, SparseCore 0:
  10.1 260.5 all-gather.4
  272.8 297.4 all-gather.2
where the time goes:
time: 887 us; the launch traced here: 886 us
  waiting for transfers between devices  552 us (62%)
  blocking collectives  187 us (21%)
  matrix products  61.8 us (7%)
  local copies, waits for them, and re-layouts  30.3 us (3%)
  other arithmetic  24.1 us (3%)
  between operations  16.7 us (2%)
    all_gather x1, waiting for transfers between devices, per_device(): lax.all_gather(image_keys, 'ctx', axis=0, tiled=True)  298 us
    all_gather x1, waiting for transfers between devices, per_device(): lax.all_gather(image_values, 'ctx', axis=0, tiled=True)  253 us
    psum x1, blocking collectives, per_device(): gate_total = lax.psum(gate_acc, ('ctx', 'tp'))  187 us
  transfers between devices with their start and end apart: 3, of which 2 were waited for; matrix products, arithmetic and copies ran while one was open for 1% of the time, Pallas kernels for 0%

commit v1 on v0

v1 whole, which is shorter than its diff:
```python
import functools
import math

import jax
import jax.numpy as jnp
from jax import lax
from jax.experimental import pallas as pl
from jax.experimental.pallas import tpu as pltpu
from jax.sharding import PartitionSpec as P

HD = 128
HEADS = 8
TOK = 256
BLK = 128
IMG = 64
SLOTS = 64
READ = 32
KEYS = READ * IMG
CHUNK = 512
RA, RB = 16, 48
X, Y, Z = 4, 2, 8
TERMS = 16384 * 8192
SCALE = math.log2(math.e) / math.sqrt(HD)
NT = (((1,), (1,)), ((), ()))
F32 = jnp.float32
BF16 = jnp.bfloat16
MESH = pl.DeviceIdType.MESH
PLANE = [(dx, dy) for dy in range(Y) for dx in range(X) if dx + dy]
VM = pl.BlockSpec(memory_space=pltpu.VMEM)
SM = pl.BlockSpec(memory_space=pltpu.SMEM)


class Place:
    def __init__(self):
        ctx = lax.axis_index("ctx")
        self.tp = lax.axis_index("tp")
        self.x = lax.rem(ctx, X)
        self.z = lax.rem(ctx // X, Z)
        self.y = ctx // (X * Z)
        self.p = self.y * X + self.x

    def z_at(self, d):
        return lax.rem(self.z + d + Z, Z)

    def p_at(self, dx, dy):
        return lax.rem(self.y + dy, Y) * X + lax.rem(self.x + dx + X, X)

    def z_dev(self, d):
        return ((self.y * Z + self.z_at(d)) * X + self.x, self.tp)

    def p_dev(self, dx, dy):
        y, x = lax.rem(self.y + dy, Y), lax.rem(self.x + dx + X, X)
        return ((y * Z + self.z) * X + x, self.tp)

    def tp_dev(self, d):
        return ((self.y * Z + self.z) * X + self.x, lax.rem(self.tp + d, 8))


def greet(devices):
    barrier = pltpu.get_barrier_semaphore()
    for dev in devices:
        pl.semaphore_signal(barrier, inc=1, device_id=dev, device_id_type=MESH)
    pl.semaphore_wait(barrier, len(devices))


class Wires:
    def __init__(self, send_sem, recv_sem):
        self.send_sem, self.recv_sem, self.sent = send_sem, recv_sem, []

    def copy(self, src, dst, dev, i):
        return pltpu.make_async_remote_copy(
            src_ref=src,
            dst_ref=dst,
            send_sem=self.send_sem.at[i],
            recv_sem=self.recv_sem.at[i],
            device_id=dev,
            device_id_type=MESH,
        )

    def send(self, src, dst, dev, i):
        one = self.copy(src, dst, dev, i)
        one.start()
        self.sent.append(one)

    def arrived(self, dst, dev, i):
        self.copy(dst, dst, dev, i).wait_recv()

    def drain(self):
        for one in self.sent:
            one.wait_send()


def gather_first(me, wires, src, ga, gb, base):
    ga[me.z * 8 + me.p] = src[0, 0:RA]
    gb[me.p * 8 + me.z] = src[0, RA:IMG]
    for d in range(1, Z):
        spot = gb.at[me.p * 8 + me.z]
        wires.send(spot, spot, me.z_dev(d), base + d)
    for i, (dx, dy) in enumerate(PLANE):
        spot = ga.at[me.z * 8 + me.p]
        wires.send(spot, spot, me.p_dev(dx, dy), base + 8 + i)


def gather_second(me, wires, ga, gb, base):
    for d in range(1, Z):
        wires.arrived(gb.at[me.p * 8 + me.z_at(-d)], me.z_dev(d), base + d)
    row = gb.at[pl.ds(me.p * 8, 8)]
    for i, (dx, dy) in enumerate(PLANE):
        wires.send(row, row, me.p_dev(dx, dy), base + 16 + i)
    for i, (dx, dy) in enumerate(PLANE):
        wires.arrived(ga.at[me.z * 8 + me.p_at(-dx, dy)], me.p_dev(dx, dy), base + 8 + i)
    row = ga.at[pl.ds(me.z * 8, 8)]
    for d in range(1, Z):
        wires.send(row, row, me.z_dev(d), base + 24 + d)


def gather_last(me, wires, ga, gb, base):
    for i, (dx, dy) in enumerate(PLANE):
        wires.arrived(gb.at[pl.ds(me.p_at(-dx, dy) * 8, 8)], me.p_dev(dx, dy), base + 16 + i)
    for d in range(1, Z):
        wires.arrived(ga.at[pl.ds(me.z_at(-d) * 8, 8)], me.z_dev(d), base + 24 + d)


def gather_kernel(k_ref, v_ref, ka, kb, va, vb, send_sem, recv_sem):
    me = Place()
    greet([me.z_dev(d) for d in range(1, Z)] + [me.p_dev(*d) for d in PLANE])
    wires = Wires(send_sem, recv_sem)
    gather_first(me, wires, k_ref, ka, kb, 0)
    gather_first(me, wires, v_ref, va, vb, 32)
    gather_second(me, wires, ka, kb, 0)
    gather_second(me, wires, va, vb, 32)
    gather_last(me, wires, ka, kb, 0)
    gather_last(me, wires, va, vb, 32)
    wires.drain()


def head_lanes(h):
    return pl.ds(pl.multiple_of(h * HD, HD), HD)


def find_reads(mask_ref, owner_ref, ids, pos):
    def image(i, n):
        slot, m0, m1 = owner_ref[i], mask_ref[0, i], mask_ref[1, i]
        read = ((m0 + m1) > 0).astype(jnp.int32)
        z, p = (slot // X) % Z, (slot // (X * Z)) * X + slot % X
        ids[0, n] = z * 8 + p
        ids[1, n] = p * 8 + z
        ids[2, n] = m0
        ids[3, n] = m1
        place = jnp.where(read > 0, n, READ)
        pos[0, z * 8 + p] = place
        pos[1, p * 8 + z] = place
        return n + read

    lax.fori_loop(0, SLOTS, image, 0)


def pick_rows(ids, a_ref, b_ref, dst, with_bias):
    lane = lax.broadcasted_iota(jnp.int32, (IMG, HD), 1)
    for j in range(READ):
        at = j * IMG
        dst[at : at + RA, 0:HD] = a_ref[ids[0, j]]
        dst[at + RA : at + IMG, 0:HD] = b_ref[ids[1, j]]
        if with_bias:
            b0 = jnp.where(ids[2, j] > 0, 0.0, -1e30)
            b1 = jnp.where(ids[3, j] > 0, 0.0, -1e30)
            bias = jnp.where(lane == 0, b0, jnp.where(lane == 1, b1, 0.0))
            dst[at : at + IMG, HD : 2 * HD] = bias.astype(BF16)


def softmax_and_values(q_ref, c_ref, kc, s_ref, p_ref, dv_ref):
    lane = lax.broadcasted_iota(jnp.int32, (TOK, HD), 1)
    row = lax.broadcasted_iota(jnp.int32, (TOK, HD), 0)
    block_of = (lane == row // BLK).astype(BF16)
    dv_ref[...] = jnp.zeros_like(dv_ref)

    def head(h, _):
        query = jnp.concatenate([q_ref[:, head_lanes(h)], block_of], axis=1)
        top = jnp.full((8, TOK), -jnp.inf, F32)
        for k in range(0, KEYS, CHUNK):
            s = lax.dot_general(kc[k : k + CHUNK, :], query, NT, preferred_element_type=F32)
            s_ref[k : k + CHUNK, :] = s
            top = jnp.maximum(top, jnp.max(s.reshape(CHUNK // 8, 8, TOK), axis=0))
        top = jnp.max(top, axis=0, keepdims=True) * SCALE
        total = jnp.zeros((8, TOK), F32)
        for k in range(0, KEYS, CHUNK):
            e = jnp.exp2(s_ref[k : k + CHUNK, :] * SCALE - top)
            total = total + jnp.sum(e.reshape(CHUNK // 8, 8, TOK), axis=0)
            s_ref[k : k + CHUNK, :] = e
        inverse = 1.0 / jnp.sum(total, axis=0, keepdims=True)
        cot = c_ref[:, head_lanes(h)]
        for k in range(0, KEYS, CHUNK):
            prob = (s_ref[k : k + CHUNK, :] * inverse).astype(BF16)
            p_ref[h, k : k + CHUNK, :] = prob
            dv_ref[k : k + CHUNK, :] += jnp.dot(prob, cot, preferred_element_type=F32)
        return 0

    lax.fori_loop(0, HEADS, head, 0)


def score_and_keys(q_ref, c_ref, vc, s_ref, p_ref, ds_ref, dk_ref, gate_ref):
    dk_ref[...] = jnp.zeros_like(dk_ref)
    gate_ref[...] = jnp.zeros_like(gate_ref)

    def head(h, _):
        cot = c_ref[:, head_lanes(h)]
        delta = jnp.zeros((8, TOK), F32)
        for k in range(0, KEYS, CHUNK):
            dp = lax.dot_general(vc[k : k + CHUNK, :], cot, NT, preferred_element_type=F32)
            s_ref[k : k + CHUNK, :] = dp
            part = dp * p_ref[h, k : k + CHUNK, :].astype(F32)
            delta = delta + jnp.sum(part.reshape(CHUNK // 8, 8, TOK), axis=0)
        gate_ref[...] += delta
        delta = jnp.sum(delta, axis=0, keepdims=True)
        query = q_ref[:, head_lanes(h)]
        for k in range(0, KEYS, CHUNK):
            prob = p_ref[h, k : k + CHUNK, :].astype(F32)
            ds = (prob * (s_ref[k : k + CHUNK, :] - delta)).astype(BF16)
            ds_ref[h, k : k + CHUNK, :] = ds
            dk_ref[k : k + CHUNK, :] += jnp.dot(ds, query, preferred_element_type=F32)
        return 0

    lax.fori_loop(0, HEADS, head, 0)


def queries_grad(kt, ds_ref, dq_ref, scale):
    def head(h, _):
        t = jnp.dot(kt[...], ds_ref[h], preferred_element_type=F32) * scale
        dq_ref[:, head_lanes(h)] = t.T.astype(BF16)
        return 0

    lax.fori_loop(0, HEADS, head, 0)


def spread_rows(pos, acc, a_ref, b_ref, scale):
    for s in range(SLOTS):
        a_ref[s] = (acc[pl.ds(pl.multiple_of(pos[0, s] * IMG, IMG), RA), :] * scale).astype(BF16)
        at = pl.multiple_of(pos[1, s] * IMG + RA, 16)
        b_ref[s] = (acc[pl.ds(at, RB), :] * scale).astype(BF16)


def local_kernel(
    mask_ref, owner_ref, gate_in, q_ref, c_ref, ka, kb, va, vb,
    dq_ref, dka, dkb, dva, dvb, gate_ref,
    ids, pos, kc, vc, kt, s_ref, p_ref, ds_ref, dk_ref, dv_ref,
):
    gate = jnp.tanh(jnp.full((1, HD), gate_in[0], F32))
    find_reads(mask_ref, owner_ref, ids, pos)
    pick_rows(ids, ka, kb, kc, True)
    pick_rows(ids, va, vb, vc, False)
    kt[...] = kc[:, 0:HD].T
    dk_ref[KEYS:, :] = jnp.zeros((IMG, HD), F32)
    dv_ref[KEYS:, :] = jnp.zeros((IMG, HD), F32)
    softmax_and_values(q_ref, c_ref, kc, s_ref, p_ref, dv_ref)
    spread_rows(pos, dv_ref, dva, dvb, gate)
    score_and_keys(q_ref, c_ref, vc, s_ref, p_ref, ds_ref, dk_ref, gate_ref)
    scale = gate * (1.0 / math.sqrt(HD))
    spread_rows(pos, dk_ref, dka, dkb, scale)
    queries_grad(kt, ds_ref, dq_ref, jnp.concatenate([scale, scale], axis=1))


def reduce_first(me, wires, sa, sb, ra, rb, base):
    for i, (dx, dy) in enumerate(PLANE):
        there = pl.ds(me.p_at(dx, dy) * 8, 8)
        wires.send(sb.at[there], rb.at[pl.ds(me.p * 8, 8)], me.p_dev(dx, dy), base + i)
    for d in range(1, Z):
        there = pl.ds(me.z_at(d) * 8, 8)
        wires.send(sa.at[there], ra.at[pl.ds(me.z * 8, 8)], me.z_dev(d), base + 8 + d)


def reduce_second(me, wires, sa, sb, ra, rb, ta, tb, ua, ub, base):
    total = sb[pl.ds(me.p * 8, 8)].astype(F32)
    for i, (dx, dy) in enumerate(PLANE):
        rows = pl.ds(me.p_at(-dx, dy) * 8, 8)
        wires.arrived(rb.at[rows], me.p_dev(dx, dy), base + i)
        total = total + rb[rows].astype(F32)
    tb[...] = total.astype(BF16)
    for d in range(1, Z):
        wires.send(tb.at[me.z_at(d)], ub.at[me.z], me.z_dev(d), base + 16 + d)
    total = sa[pl.ds(me.z * 8, 8)].astype(F32)
    for d in range(1, Z):
        rows = pl.ds(me.z_at(-d) * 8, 8)
        wires.arrived(ra.at[rows], me.z_dev(d), base + 8 + d)
        total = total + ra[rows].astype(F32)
    ta[...] = total.astype(BF16)
    for i, (dx, dy) in enumerate(PLANE):
        wires.send(ta.at[me.p_at(dx, dy)], ua.at[me.p], me.p_dev(dx, dy), base + 24 + i)


def reduce_last(me, wires, ta, tb, ua, ub, out, base):
    total = tb[me.z].astype(F32)
    for d in range(1, Z):
        wires.arrived(ub.at[me.z_at(-d)], me.z_dev(d), base + 16 + d)
        total = total + ub[me.z_at(-d)].astype(F32)
    out[0, RA:IMG] = total.astype(BF16)
    total = ta[me.p].astype(F32)
    for i, (dx, dy) in enumerate(PLANE):
        wires.arrived(ua.at[me.p_at(-dx, dy)], me.p_dev(dx, dy), base + 24 + i)
        total = total + ua[me.p_at(-dx, dy)].astype(F32)
    out[0, 0:RA] = total.astype(BF16)


def gate_step(wires, own, box, devices, places, base):
    for i, dev in enumerate(devices):
        wires.send(own, box.at[i], dev, base + i)

    def finish():
        total = own[...]
        for i, dev in enumerate(devices):
            wires.arrived(box.at[i], dev, base + i)
            total = total + box[i]
        return total

    return finish


def reduce_kernel(
    gate_in, dka, dkb, dva, dvb, gate_part, dk_out, dv_out, gate_out,
    rka, rkb, rva, rvb, tka, tkb, tva, tvb, uka, ukb, uva, uvb, gate_own, gate_box, send_sem, recv_sem,
):
    me = Place()
    along_z = [me.z_dev(d) for d in range(1, Z)]
    in_plane = [me.p_dev(*d) for d in PLANE]
    along_tp = [me.tp_dev(d) for d in range(1, 8)]
    greet(along_z + in_plane + along_tp)
    wires = Wires(send_sem, recv_sem)
    gate_own[0] = gate_part[:, 0:HD] + gate_part[:, HD : 2 * HD]
    step = gate_step(wires, gate_own.at[0], gate_box.at[0], along_z, None, 64)
    reduce_first(me, wires, dva, dvb, rva, rvb, 0)
    reduce_first(me, wires, dka, dkb, rka, rkb, 32)
    gate_own[1] = step()
    step = gate_step(wires, gate_own.at[1], gate_box.at[1], in_plane, None, 71)
    reduce_second(me, wires, dva, dvb, rva, rvb, tva, tvb, uva, uvb, 0)
    gate_own[2] = step()
    step = gate_step(wires, gate_own.at[2], gate_box.at[2], along_tp, None, 78)
    reduce_second(me, wires, dka, dkb, rka, rkb, tka, tkb, uka, ukb, 32)
    reduce_last(me, wires, tva, tvb, uva, uvb, dv_out, 0)
    reduce_last(me, wires, tka, tkb, uka, ukb, dk_out, 32)
    gate = jnp.tanh(jnp.full((8, HD), gate_in[0], F32))
    gate_out[0] = jnp.sum((1.0 - gate * gate) * step()) * (1.0 / math.sqrt(TERMS))
    wires.drain()


def per_device(queries, cotangent, image_keys, image_values, attn_gate, block_mask, image_owner):
    shape = jax.ShapeDtypeStruct
    rows_a, rows_b = shape((SLOTS, RA, HD), BF16), shape((SLOTS, RB, HD), BF16)
    dma = pltpu.SemaphoreType.DMA
    gathered = pl.pallas_call(
        gather_kernel,
        out_shape=[rows_a, rows_b, rows_a, rows_b],
        in_specs=[VM] * 2,
        out_specs=[VM] * 4,
        scratch_shapes=[dma((64,))] * 2,
        compiler_params=pltpu.CompilerParams(
            collective_id=0, has_side_effects=True, vmem_limit_bytes=16 << 20
        ),
    )(image_keys, image_values)
    dq, dka, dkb, dva, dvb, gate_part = pl.pallas_call(
        local_kernel,
        out_shape=[shape((TOK, HEADS * HD), BF16), rows_a, rows_b, rows_a, rows_b, shape((8, TOK), F32)],
        in_specs=[SM] * 3 + [VM] * 6,
        out_specs=[VM] * 6,
        scratch_shapes=[
            pltpu.SMEM((4, READ + 1), jnp.int32),
            pltpu.SMEM((2, SLOTS), jnp.int32),
            pltpu.VMEM((KEYS, 2 * HD), BF16),
            pltpu.VMEM((KEYS, HD), BF16),
            pltpu.VMEM((HD, KEYS), BF16),
            pltpu.VMEM((KEYS, TOK), F32),
            pltpu.VMEM((HEADS, KEYS, TOK), BF16),
            pltpu.VMEM((HEADS, KEYS, TOK), BF16),
            pltpu.VMEM((KEYS + IMG, HD), F32),
            pltpu.VMEM((KEYS + IMG, HD), F32),
        ],
        compiler_params=pltpu.CompilerParams(vmem_limit_bytes=48 << 20),
    )(block_mask, image_owner, attn_gate, queries, cotangent, *gathered)
    part_a, part_b = pltpu.VMEM((8, RA, HD), BF16), pltpu.VMEM((8, RB, HD), BF16)
    whole_a, whole_b = pltpu.VMEM((SLOTS, RA, HD), BF16), pltpu.VMEM((SLOTS, RB, HD), BF16)
    grad = shape((1, IMG, HD), BF16)
    dk, dv, gate = pl.pallas_call(
        reduce_kernel,
        out_shape=[grad, grad, shape((1,), F32)],
        in_specs=[SM] + [VM] * 5,
        out_specs=[VM, VM, SM],
        scratch_shapes=[whole_a, whole_b] * 2
        + [part_a, part_b] * 4
        + [pltpu.VMEM((3, 8, HD), F32), pltpu.VMEM((3, 7, 8, HD), F32), dma((88,)), dma((88,))],
        compiler_params=pltpu.CompilerParams(
            collective_id=1, has_side_effects=True, vmem_limit_bytes=24 << 20
        ),
    )(attn_gate, dka, dkb, dva, dvb, gate_part)
    return dq, dk, dv, gate


def solution(mesh):
    specs = (P("ctx", "tp"), P("ctx", "tp"), P("ctx", None, "tp"), P("ctx", None, "tp"), P(), P("ctx", None), P())
    outs = (P("ctx", "tp"), P("ctx", None, "tp"), P("ctx", None, "tp"), P())
    return jax.shard_map(per_device, mesh=mesh, in_specs=specs, out_specs=outs, check_vma=False)
```

time: 887 us -> 105 us (0.12)
  waiting for transfers between devices: 552 us -> 0 us
  blocking collectives: 187 us -> 0 us
  Pallas kernels: 0 us -> 96.2 us
  matrix products: 61.8 us -> 0 us
  local copies, waits for them, and re-layouts: 30.3 us -> 5.39 us
  other arithmetic: 24.1 us -> 0 us
  between operations: 16.7 us -> 3.13 us
    all_gather x2 -> x0, waiting for transfers between devices: 551 us -> none  [the longest x1 298 us: per_device(): lax.all_gather(image_keys, 'ctx', axis=0, tiled=True)]
    psum x1 -> x0, blocking collectives: 187 us -> none  [per_device(): gate_total = lax.psum(gate_acc, ('ctx', 'tp'))]
    pallas_call x0 -> x3, Pallas kernels: none -> 96.2 us  [the longest x1 36.5 us: per_device(): pl.pallas_call(reduce_kernel, out_shape=[grad, grad, shape((1,), F32)], i...]
    dot_general x48 -> x0, matrix products: 61.8 us -> none  [the longest x8 15.5 us: head_step(): jnp.einsum('kts,skd->tkd', prob_half, value_rows, preferred_element_type=...]
    while x98 -> x0, local copies, waits for them, and re-layouts: 11 us -> none
  transfers between devices with their start and end apart: 3 -> 0, of which waited for: 2 -> 0; matrix products, arithmetic and copies ran while one was open for 1% -> 0% of each run, Pallas kernels for 0% -> 0%
where the time goes in v1:
time: 105 us
  Pallas kernels  96.2 us (92%)
  local copies, waits for them, and re-layouts  5.39 us (5%)
  between operations  3.13 us (3%)
    pallas_call x1, Pallas kernels, per_device(): pl.pallas_call(reduce_kernel, out_shape=[grad, grad, shape((1,), F32)], i...  36.5 us
    pallas_call x1, Pallas kernels, per_device(): pl.pallas_call(gather_kernel, out_shape=[rows_a, rows_b, rows_a, rows_b],...  35.3 us
    pallas_call x1, Pallas kernels, per_device(): pl.pallas_call(local_kernel, out_shape=[shape((TOK, HEADS * HD), BF16), r...  24.4 us
    unnamed x14, local copies, waits for them, and re-layouts  5.39 us

profile of v1, /device:TPU:1, one launch (start us, length us, event | category | flops | bytes accessed | tf_op | source)
XLA Modules:
  0.0 104.7 jit_solution(863393960407593581)
XLA Ops:
  1.3 0.0 copy-start.2
  1.3 0.7 copy-done.2
  2.0 0.0 copy-start.3
  2.0 0.7 copy-done.3
  2.7 35.3 %shard_map.102 = (bf16[64,16,128]{2,1,0:T(8,128)(2,1)S(1)}, bf16[64,48,128]{2,1,0:T(8,128)(2,1)S(1)}, bf16[64,16,128]{2,1,0:T(8,128)(2,1)S(1)}, bf16[64,48,128]{2,1,0:T(8,128)(2,1)S(1)}) custom-call(bf16[1,64,128]{2,1,0:T(8,128)(2,1)S(1)} %copy-done.2, bf16[1,64,128]{2,1,0:T(8,128)(2,1)S(1)} %copy-done.3), custom_call_target="tpu_custom_call" | custom-call | tf_op jit(solution)/shard_map/pallas_call | solution.py:348
  38.0 0.0 copy-start.4
  38.0 0.0 copy-start.5
  38.0 0.7 copy-done.4
  38.7 0.0 copy-done.5
  38.7 0.0 copy-start
  38.7 1.0 copy-done
  39.7 0.0 copy-start.1
  39.7 1.0 copy-done.1
  40.8 24.4 %shard_map.103 = (bf16[256,1024]{1,0:T(8,128)(2,1)}, bf16[64,16,128]{2,1,0:T(8,128)(2,1)S(1)}, bf16[64,48,128]{2,1,0:T(8,128)(2,1)S(1)}, bf16[64,16,128]{2,1,0:T...) custom-call(s32[2,64]{1,0:T(2,128)S(1)} %copy-done.4, s32[64]{0:T(128)S(1)} %copy-done.5, ...), custom_call_target="tpu_custom_call" | custom-call | tf_op jit(solution)/shard_map/pallas_call | solution.py:358
  65.2 36.5 %shard_map.104 = (bf16[1,64,128]{2,1,0:T(8,128)(2,1)S(1)}, bf16[1,64,128]{2,1,0:T(8,128)(2,1)S(1)}, f32[1]{0:T(128)}) custom-call(f32[1]{0:T(128)S(6)} %copy.14.gate_in, bf16[64,16,128]{2,1,0:T(8,128)(2,1)S(1)} %get-tuple-element.22.dka, bf16[64,48,128]{2,1,0:T(8,128)(2,1)S(1)} %get-tuple-element.23.dkb, bf16[64,16,128]{2,1,0:T(8,128)(2,1)S(1)} %get-tuple-element.24.dva, ...), custom_call_target="tpu_custom_call" | custom-call | tf_op jit(solution)/shard_map/pallas_call | solution.py:380
  101.7 0.6 copy.15
  102.3 0.6 copy.16
Async XLA Ops:
  1.3 0.7 copy-start.2
  2.0 0.7 copy-start.3
  38.0 0.7 copy-start.4
  38.0 0.7 copy-start.5
  38.7 1.0 copy-start
  39.7 1.0 copy-start.1

commit v2 on v1

--- a/solution.py
+++ b/solution.py
@@ -91,14 +91,10 @@
 
 
 def gather_first(me, wires, src, ga, gb, base):
-    ga[me.z * 8 + me.p] = src[0, 0:RA]
-    gb[me.p * 8 + me.z] = src[0, RA:IMG]
-    for d in range(1, Z):
-        spot = gb.at[me.p * 8 + me.z]
-        wires.send(spot, spot, me.z_dev(d), base + d)
-    for i, (dx, dy) in enumerate(PLANE):
-        spot = ga.at[me.z * 8 + me.p]
-        wires.send(spot, spot, me.p_dev(dx, dy), base + 8 + i)
+    for d in range(1, Z):
+        wires.send(src.at[0, RA:IMG], gb.at[me.p * 8 + me.z], me.z_dev(d), base + d)
+    for i, (dx, dy) in enumerate(PLANE):
+        wires.send(src.at[0, 0:RA], ga.at[me.z * 8 + me.p], me.p_dev(dx, dy), base + 8 + i)
 
 
 def gather_second(me, wires, ga, gb, base):
@@ -121,49 +117,44 @@
         wires.arrived(ga.at[pl.ds(me.z_at(-d) * 8, 8)], me.z_dev(d), base + 24 + d)
 
 
-def gather_kernel(k_ref, v_ref, ka, kb, va, vb, send_sem, recv_sem):
-    me = Place()
-    greet([me.z_dev(d) for d in range(1, Z)] + [me.p_dev(*d) for d in PLANE])
-    wires = Wires(send_sem, recv_sem)
-    gather_first(me, wires, k_ref, ka, kb, 0)
-    gather_first(me, wires, v_ref, va, vb, 32)
-    gather_second(me, wires, ka, kb, 0)
-    gather_second(me, wires, va, vb, 32)
-    gather_last(me, wires, ka, kb, 0)
-    gather_last(me, wires, va, vb, 32)
-    wires.drain()
-
-
 def head_lanes(h):
     return pl.ds(pl.multiple_of(h * HD, HD), HD)
 
 
-def find_reads(mask_ref, owner_ref, ids, pos):
-    def image(i, n):
-        slot, m0, m1 = owner_ref[i], mask_ref[0, i], mask_ref[1, i]
-        read = ((m0 + m1) > 0).astype(jnp.int32)
-        z, p = (slot // X) % Z, (slot // (X * Z)) * X + slot % X
-        ids[0, n] = z * 8 + p
-        ids[1, n] = p * 8 + z
-        ids[2, n] = m0
-        ids[3, n] = m1
-        place = jnp.where(read > 0, n, READ)
-        pos[0, z * 8 + p] = place
-        pos[1, p * 8 + z] = place
-        return n + read
-
-    lax.fori_loop(0, SLOTS, image, 0)
-
-
-def pick_rows(ids, a_ref, b_ref, dst, with_bias):
+def find_reads(mask_ref, owner_ref, table):
+    down = lax.broadcasted_iota(jnp.int32, (SLOTS, HD), 0)
+    across = lax.broadcasted_iota(jnp.int32, (SLOTS, HD), 1)
+
+    def image(i, reads):
+        slot = owner_ref[i]
+        hit = down == ((slot // X) % Z) * 8 + (slot // (X * Z)) * X + slot % X
+        return tuple(jnp.where(hit, mask_ref[b, i], r) for b, r in enumerate(reads))
+
+    def total(where, what):
+        return jnp.sum(jnp.where(where, what, 0), axis=0, keepdims=True)
+
+    zero = jnp.zeros((SLOTS, HD), jnp.int32)
+    first, second = lax.fori_loop(0, SLOTS, image, (zero, zero))
+    read = jnp.minimum(first + second, 1)
+    position = jnp.where(total(down == across, read) > 0, total(down < across, read), READ)
+    chosen = jnp.broadcast_to(position, (HD, HD)).T[0:SLOTS] == across
+    sub = lax.broadcasted_iota(jnp.int32, (8, HD), 0)
+    low = jnp.where(sub == 0, total(chosen, down), total(chosen, first))
+    high = jnp.where(sub == 2, total(chosen, second), position)
+    turned = lax.rem(down, 8) * 8 + down // 8
+    table[...] = jnp.where(sub < 2, low, jnp.where(sub < 4, high, total(chosen, turned)))
+
+
+def pick_rows(table, a_ref, b_ref, dst, with_bias):
     lane = lax.broadcasted_iota(jnp.int32, (IMG, HD), 1)
     for j in range(READ):
         at = j * IMG
-        dst[at : at + RA, 0:HD] = a_ref[ids[0, j]]
-        dst[at + RA : at + IMG, 0:HD] = b_ref[ids[1, j]]
+        place = table[0, j]
+        dst[at : at + RA, 0:HD] = a_ref[place]
+        dst[at + RA : at + IMG, 0:HD] = b_ref[table[4, j]]
         if with_bias:
-            b0 = jnp.where(ids[2, j] > 0, 0.0, -1e30)
-            b1 = jnp.where(ids[3, j] > 0, 0.0, -1e30)
+            b0 = jnp.where(table[1, j] > 0, 0.0, -1e30)
+            b1 = jnp.where(table[2, j] > 0, 0.0, -1e30)
             bias = jnp.where(lane == 0, b0, jnp.where(lane == 1, b1, 0.0))
             dst[at : at + IMG, HD : 2 * HD] = bias.astype(BF16)
 
@@ -192,7 +183,8 @@
         for k in range(0, KEYS, CHUNK):
             prob = (s_ref[k : k + CHUNK, :] * inverse).astype(BF16)
             p_ref[h, k : k + CHUNK, :] = prob
-            dv_ref[k : k + CHUNK, :] += jnp.dot(prob, cot, preferred_element_type=F32)
+            part = jnp.dot(prob, cot, preferred_element_type=F32)
+            dv_ref[k // IMG : (k + CHUNK) // IMG] += part.reshape(CHUNK // IMG, IMG, HD)
         return 0
 
     lax.fori_loop(0, HEADS, head, 0)
@@ -217,7 +209,8 @@
             prob = p_ref[h, k : k + CHUNK, :].astype(F32)
             ds = (prob * (s_ref[k : k + CHUNK, :] - delta)).astype(BF16)
             ds_ref[h, k : k + CHUNK, :] = ds
-            dk_ref[k : k + CHUNK, :] += jnp.dot(ds, query, preferred_element_type=F32)
+            part = jnp.dot(ds, query, preferred_element_type=F32)
+            dk_ref[k // IMG : (k + CHUNK) // IMG] += part.reshape(CHUNK // IMG, IMG, HD)
         return 0
 
     lax.fori_loop(0, HEADS, head, 0)
@@ -232,31 +225,10 @@
     lax.fori_loop(0, HEADS, head, 0)
 
 
-def spread_rows(pos, acc, a_ref, b_ref, scale):
+def spread_rows(table, acc, a_ref, b_ref, scale):
     for s in range(SLOTS):
-        a_ref[s] = (acc[pl.ds(pl.multiple_of(pos[0, s] * IMG, IMG), RA), :] * scale).astype(BF16)
-        at = pl.multiple_of(pos[1, s] * IMG + RA, 16)
-        b_ref[s] = (acc[pl.ds(at, RB), :] * scale).astype(BF16)
-
-
-def local_kernel(
-    mask_ref, owner_ref, gate_in, q_ref, c_ref, ka, kb, va, vb,
-    dq_ref, dka, dkb, dva, dvb, gate_ref,
-    ids, pos, kc, vc, kt, s_ref, p_ref, ds_ref, dk_ref, dv_ref,
-):
-    gate = jnp.tanh(jnp.full((1, HD), gate_in[0], F32))
-    find_reads(mask_ref, owner_ref, ids, pos)
-    pick_rows(ids, ka, kb, kc, True)
-    pick_rows(ids, va, vb, vc, False)
-    kt[...] = kc[:, 0:HD].T
-    dk_ref[KEYS:, :] = jnp.zeros((IMG, HD), F32)
-    dv_ref[KEYS:, :] = jnp.zeros((IMG, HD), F32)
-    softmax_and_values(q_ref, c_ref, kc, s_ref, p_ref, dv_ref)
-    spread_rows(pos, dv_ref, dva, dvb, gate)
-    score_and_keys(q_ref, c_ref, vc, s_ref, p_ref, ds_ref, dk_ref, gate_ref)
-    scale = gate * (1.0 / math.sqrt(HD))
-    spread_rows(pos, dk_ref, dka, dkb, scale)
-    queries_grad(kt, ds_ref, dq_ref, jnp.concatenate([scale, scale], axis=1))
+        a_ref[s] = (acc[table[3, s], 0:RA] * scale).astype(BF16)
+        b_ref[s] = (acc[table[3, (s % 8) * 8 + s // 8], RA:IMG] * scale).astype(BF16)
 
 
 def reduce_first(me, wires, sa, sb, ra, rb, base):
@@ -300,7 +272,7 @@
     out[0, 0:RA] = total.astype(BF16)
 
 
-def gate_step(wires, own, box, devices, places, base):
+def gate_step(wires, own, box, devices, base):
     for i, dev in enumerate(devices):
         wires.send(own, box.at[i], dev, base + i)
 
@@ -314,82 +286,125 @@
     return finish
 
 
-def reduce_kernel(
-    gate_in, dka, dkb, dva, dvb, gate_part, dk_out, dv_out, gate_out,
-    rka, rkb, rva, rvb, tka, tkb, tva, tvb, uka, ukb, uva, uvb, gate_own, gate_box, send_sem, recv_sem,
+def kernel(
+    mask_in, owner_in, gate_in, q_in, c_in, k_in, v_in, dq_out, dk_out, dv_out, gate_out,
+    mask_ref, owner_ref, gate_ref, table_v, table, q_ref, c_ref, dq_ref,
+    ka, kb, va, vb, kc, vc, kt, s_ref, p_ref, ds_ref, dk_ref, dv_ref,
+    dka, dkb, dva, dvb, rka, rkb, rva, rvb, tka, tkb, tva, tvb, uka, ukb, uva, uvb,
+    gate_rows, gate_own, gate_box, local_sem, send_sem, recv_sem,
 ):
     me = Place()
     along_z = [me.z_dev(d) for d in range(1, Z)]
     in_plane = [me.p_dev(*d) for d in PLANE]
     along_tp = [me.tp_dev(d) for d in range(1, 8)]
+    here_a, here_b = me.z * 8 + me.p, me.p * 8 + me.z
+    inputs = [
+        pltpu.make_async_copy(src, dst, local_sem.at[i])
+        for i, (src, dst) in enumerate(
+            (
+                (k_in.at[0, 0:RA], ka.at[here_a]),
+                (k_in.at[0, RA:IMG], kb.at[here_b]),
+                (v_in.at[0, 0:RA], va.at[here_a]),
+                (v_in.at[0, RA:IMG], vb.at[here_b]),
+                (mask_in, mask_ref),
+                (owner_in, owner_ref),
+                (gate_in, gate_ref),
+                (q_in, q_ref),
+                (c_in, c_ref),
+            )
+        )
+    ]
+    for one in inputs:
+        one.start()
     greet(along_z + in_plane + along_tp)
     wires = Wires(send_sem, recv_sem)
-    gate_own[0] = gate_part[:, 0:HD] + gate_part[:, HD : 2 * HD]
-    step = gate_step(wires, gate_own.at[0], gate_box.at[0], along_z, None, 64)
-    reduce_first(me, wires, dva, dvb, rva, rvb, 0)
-    reduce_first(me, wires, dka, dkb, rka, rkb, 32)
+    gather_first(me, wires, k_in, ka, kb, 0)
+    gather_first(me, wires, v_in, va, vb, 32)
+    for one in inputs:
+        one.wait()
+    gate = jnp.tanh(jnp.full((1, HD), gate_ref[0], F32))
+    find_reads(mask_ref, owner_ref, table_v)
+    put = pltpu.make_async_copy(table_v, table, local_sem.at[9])
+    put.start()
+    dk_ref[READ] = jnp.zeros((IMG, HD), F32)
+    dv_ref[READ] = jnp.zeros((IMG, HD), F32)
+    put.wait()
+    gather_second(me, wires, ka, kb, 0)
+    gather_last(me, wires, ka, kb, 0)
+    gather_second(me, wires, va, vb, 32)
+    pick_rows(table, ka, kb, kc, True)
+    kt[...] = kc[:, 0:HD].T
+    softmax_and_values(q_ref, c_ref, kc, s_ref, p_ref, dv_ref)
+    spread_rows(table, dv_ref, dva, dvb, gate)
+    reduce_first(me, wires, dva, dvb, rva, rvb, 64)
+    gather_last(me, wires, va, vb, 32)
+    pick_rows(table, va, vb, vc, False)
+    score_and_keys(q_ref, c_ref, vc, s_ref, p_ref, ds_ref, dk_ref, gate_rows)
+    scale = gate * (1.0 / math.sqrt(HD))
+    spread_rows(table, dk_ref, dka, dkb, scale)
+    reduce_first(me, wires, dka, dkb, rka, rkb, 96)
+    gate_own[0] = gate_rows[:, 0:HD] + gate_rows[:, HD : 2 * HD]
+    step = gate_step(wires, gate_own.at[0], gate_box.at[0], along_z, 128)
+    reduce_second(me, wires, dva, dvb, rva, rvb, tva, tvb, uva, uvb, 64)
+    queries_grad(kt, ds_ref, dq_ref, jnp.concatenate([scale, scale], axis=1))
+    back = pltpu.make_async_copy(dq_ref, dq_out, local_sem.at[10])
+    back.start()
     gate_own[1] = step()
-    step = gate_step(wires, gate_own.at[1], gate_box.at[1], in_plane, None, 71)
-    reduce_second(me, wires, dva, dvb, rva, rvb, tva, tvb, uva, uvb, 0)
+    step = gate_step(wires, gate_own.at[1], gate_box.at[1], in_plane, 135)
+    reduce_last(me, wires, tva, tvb, uva, uvb, dv_out, 64)
     gate_own[2] = step()
-    step = gate_step(wires, gate_own.at[2], gate_box.at[2], along_tp, None, 78)
-    reduce_second(me, wires, dka, dkb, rka, rkb, tka, tkb, uka, ukb, 32)
-    reduce_last(me, wires, tva, tvb, uva, uvb, dv_out, 0)
-    reduce_last(me, wires, tka, tkb, uka, ukb, dk_out, 32)
-    gate = jnp.tanh(jnp.full((8, HD), gate_in[0], F32))
+    step = gate_step(wires, gate_own.at[2], gate_box.at[2], along_tp, 142)
+    reduce_second(me, wires, dka, dkb, rka, rkb, tka, tkb, uka, ukb, 96)
+    gate = jnp.tanh(jnp.full((8, HD), gate_ref[0], F32))
     gate_out[0] = jnp.sum((1.0 - gate * gate) * step()) * (1.0 / math.sqrt(TERMS))
+    reduce_last(me, wires, tka, tkb, uka, ukb, dk_out, 96)
+    back.wait()
     wires.drain()
 
 
 def per_device(queries, cotangent, image_keys, image_values, attn_gate, block_mask, image_owner):
     shape = jax.ShapeDtypeStruct
-    rows_a, rows_b = shape((SLOTS, RA, HD), BF16), shape((SLOTS, RB, HD), BF16)
     dma = pltpu.SemaphoreType.DMA
-    gathered = pl.pallas_call(
-        gather_kernel,
-        out_shape=[rows_a, rows_b, rows_a, rows_b],
-        in_specs=[VM] * 2,
-        out_specs=[VM] * 4,
-        scratch_shapes=[dma((64,))] * 2,
-        compiler_params=pltpu.CompilerParams(
-            collective_id=0, has_side_effects=True, vmem_limit_bytes=16 << 20
-        ),
-    )(image_keys, image_values)
-    dq, dka, dkb, dva, dvb, gate_part = pl.pallas_call(
-        local_kernel,
-        out_shape=[shape((TOK, HEADS * HD), BF16), rows_a, rows_b, rows_a, rows_b, shape((8, TOK), F32)],
-        in_specs=[SM] * 3 + [VM] * 6,
-        out_specs=[VM] * 6,
+    rows = shape((TOK, HEADS * HD), BF16)
+    rows_here = pltpu.VMEM((TOK, HEADS * HD), BF16)
+    part_a, part_b = pltpu.VMEM((8, RA, HD), BF16), pltpu.VMEM((8, RB, HD), BF16)
+    whole_a, whole_b = pltpu.VMEM((SLOTS, RA, HD), BF16), pltpu.VMEM((SLOTS, RB, HD), BF16)
+    grad = shape((1, IMG, HD), BF16)
+    anywhere = pl.BlockSpec(memory_space=pltpu.HBM)
+    return pl.pallas_call(
+        kernel,
+        out_shape=[rows, grad, grad, shape((1,), F32)],
+        in_specs=[anywhere] * 7,
+        out_specs=[anywhere, VM, VM, SM],
         scratch_shapes=[
-            pltpu.SMEM((4, READ + 1), jnp.int32),
             pltpu.SMEM((2, SLOTS), jnp.int32),
+            pltpu.SMEM((SLOTS,), jnp.int32),
+            pltpu.SMEM((1,), F32),
+            pltpu.VMEM((8, HD), jnp.int32),
+            pltpu.SMEM((8, HD), jnp.int32),
+            rows_here,
+            rows_here,
+            rows_here,
+        ]
+        + [whole_a, whole_b] * 2
+        + [
             pltpu.VMEM((KEYS, 2 * HD), BF16),
             pltpu.VMEM((KEYS, HD), BF16),
             pltpu.VMEM((HD, KEYS), BF16),
             pltpu.VMEM((KEYS, TOK), F32),
             pltpu.VMEM((HEADS, KEYS, TOK), BF16),
             pltpu.VMEM((HEADS, KEYS, TOK), BF16),
-            pltpu.VMEM((KEYS + IMG, HD), F32),
-            pltpu.VMEM((KEYS + IMG, HD), F32),
-        ],
-        compiler_params=pltpu.CompilerParams(vmem_limit_bytes=48 << 20),
-    )(block_mask, image_owner, attn_gate, queries, cotangent, *gathered)
-    part_a, part_b = pltpu.VMEM((8, RA, HD), BF16), pltpu.VMEM((8, RB, HD), BF16)
-    whole_a, whole_b = pltpu.VMEM((SLOTS, RA, HD), BF16), pltpu.VMEM((SLOTS, RB, HD), BF16)
-    grad = shape((1, IMG, HD), BF16)
-    dk, dv, gate = pl.pallas_call(
-        reduce_kernel,
-        out_shape=[grad, grad, shape((1,), F32)],
-        in_specs=[SM] + [VM] * 5,
-        out_specs=[VM, VM, SM],
-        scratch_shapes=[whole_a, whole_b] * 2
+            pltpu.VMEM((READ + 1, IMG, HD), F32),
+            pltpu.VMEM((READ + 1, IMG, HD), F32),
+        ]
+        + [whole_a, whole_b] * 4
         + [part_a, part_b] * 4
-        + [pltpu.VMEM((3, 8, HD), F32), pltpu.VMEM((3, 7, 8, HD), F32), dma((88,)), dma((88,))],
+        + [pltpu.VMEM((8, TOK), F32), pltpu.VMEM((3, 8, HD), F32), pltpu.VMEM((3, 7, 8, HD), F32)]
+        + [dma((11,)), dma((150,)), dma((150,))],
         compiler_params=pltpu.CompilerParams(
-            collective_id=1, has_side_effects=True, vmem_limit_bytes=24 << 20
+            collective_id=0, has_side_effects=True, vmem_limit_bytes=(64 << 20) - (64 << 10)
         ),
-    )(attn_gate, dka, dkb, dva, dvb, gate_part)
-    return dq, dk, dv, gate
+    )(block_mask, image_owner, attn_gate, queries, cotangent, image_keys, image_values)
 
 
 def solution(mesh):

time: 105 us -> 77.9 us (0.74)
  Pallas kernels: 96.2 us -> 70.8 us
  local copies, waits for them, and re-layouts: 5.39 us -> 3.21 us
    pallas_call x3 -> x1, Pallas kernels: 96.2 us -> 70.8 us  [per_device(): pl.pallas_call(kernel, out_shape=[rows, grad, grad, shape((1,), F32)], in...]
    unnamed x14 -> x7, local copies, waits for them, and re-layouts: 5.39 us -> 3.21 us
where the time goes in v2:
time: 77.9 us; the launch traced here: 77.1 us
  Pallas kernels  70.8 us (91%)
  local copies, waits for them, and re-layouts  3.21 us (4%)
  between operations  3.1 us (4%)
    pallas_call x1, Pallas kernels, per_device(): pl.pallas_call(kernel, out_shape=[rows, grad, grad, shape((1,), F32)], in...  70.8 us
    unnamed x7, local copies, waits for them, and re-layouts  3.21 us

profile of v2, /device:TPU:1, one launch (start us, length us, event | category | flops | bytes accessed | tf_op | source)
XLA Modules:
  0.0 77.1 jit_solution(7441810381106458980)
XLA Ops:
  1.3 70.8 %shard_map.102 = (bf16[256,1024]{1,0:T(8,128)(2,1)}, bf16[1,64,128]{2,1,0:T(8,128)(2,1)}, bf16[1,64,128]{2,1,0:T(8,128)(2,1)}, f32[1]{0:T(128)}) custom-call(s32[2,64]{1,0:T(2,128)} %mask_in.1, s32[64]{0:T(128)} %owner_in.1, f32[1]{0:T(128)S(6)} %copy.15.gate_in, bf16[256,1024]{1,0:T(8,128)(2,1)} %q_in.1, bf16[256,1024]{1,0:T(8,128)(2,1)} %c_in.1, ...), custom_call_target="tpu_custom_call" | custom-call | tf_op jit(solution)/shard_map/pallas_call | solution.py:374
  72.1 0.0 copy-start.1
  72.1 1.9 %copy.16 = bf16[256,1024]{1,0:T(8,128)(2,1)} copy(bf16[256,1024]{1,0:T(8,128)(2,1)} %get-tuple-element.8) | data formatting | bytes 1048576
  74.0 0.0 copy-done.1
  74.0 0.0 copy-start
  74.0 0.6 copy.17
  74.6 0.1 copy-done
  74.7 0.6 copy.18
Async XLA Ops:
  72.1 1.9 %copy-start.1 = (bf16[1,64,128]{2,1,0:T(8,128)(2,1)S(1)}, bf16[1,64,128]{2,1,0:T(8,128)(2,1)}, u32[]{:S(2)}) copy-start(bf16[1,64,128]{2,1,0:T(8,128)(2,1)} %get-tuple-element.9) | copy-start | bytes 49156
  74.0 0.7 copy-start

commit v3 on v2

v3 whole, which is shorter than its diff:
```python
import functools
import math

import jax
import jax.numpy as jnp
from jax import lax
from jax.experimental import pallas as pl
from jax.experimental.pallas import tpu as pltpu
from jax.sharding import PartitionSpec as P

HD = 128
HEADS = 8
TOK = 256
BLK = 128
IMG = 64
SLOTS = 64
READ = 32
KEYS = READ * IMG
CHUNK = 512
TOGETHER = 4
RA, RB = 16, 48
X, Y, Z = 4, 2, 8
TERMS = 16384 * 8192
SCALE = math.log2(math.e) / math.sqrt(HD)
NT = (((1,), (1,)), ((), ()))
F32 = jnp.float32
BF16 = jnp.bfloat16
MESH = pl.DeviceIdType.MESH
PLANE = [(dx, dy) for dy in range(Y) for dx in range(X) if dx + dy]
VM = pl.BlockSpec(memory_space=pltpu.VMEM)
SM = pl.BlockSpec(memory_space=pltpu.SMEM)


class Place:
    def __init__(self):
        ctx = lax.axis_index("ctx")
        self.tp = lax.axis_index("tp")
        self.x = lax.rem(ctx, X)
        self.z = lax.rem(ctx // X, Z)
        self.y = ctx // (X * Z)
        self.p = self.y * X + self.x

    def z_at(self, d):
        return lax.rem(self.z + d + Z, Z)

    def p_at(self, dx, dy):
        return lax.rem(self.y + dy, Y) * X + lax.rem(self.x + dx + X, X)

    def z_dev(self, d):
        return ((self.y * Z + self.z_at(d)) * X + self.x, self.tp)

    def p_dev(self, dx, dy):
        y, x = lax.rem(self.y + dy, Y), lax.rem(self.x + dx + X, X)
        return ((y * Z + self.z) * X + x, self.tp)

    def tp_dev(self, d):
        return ((self.y * Z + self.z) * X + self.x, lax.rem(self.tp + d, 8))


def greet(devices):
    barrier = pltpu.get_barrier_semaphore()
    for dev in devices:
        pl.semaphore_signal(barrier, inc=1, device_id=dev, device_id_type=MESH)
    pl.semaphore_wait(barrier, len(devices))


class Wires:
    def __init__(self, send_sem, recv_sem):
        self.send_sem, self.recv_sem, self.groups, self.gone = send_sem, recv_sem, {}, []

    def copy(self, src, dst, dev, group):
        return pltpu.make_async_remote_copy(
            src_ref=src,
            dst_ref=dst,
            send_sem=self.send_sem.at[group],
            recv_sem=self.recv_sem.at[group],
            device_id=dev,
            device_id_type=MESH,
        )

    def send(self, src, dst, dev, group):
        self.copy(src, dst, dev, group).start()

    def arrived(self, whole, dev, group):
        one = self.copy(whole, whole, dev, group)
        one.wait_recv()
        self.groups[group] = one

    def left(self, whole, dev, group):
        self.copy(whole, whole, dev, group).wait_send()
        self.gone.append(group)

    def drain(self):
        for group, one in self.groups.items():
            if group not in self.gone:
                one.wait_send()


def gather_first(me, wires, src, ga, gb, base):
    for d in range(1, Z):
        wires.send(src.at[0, RA:IMG], gb.at[me.p * 8 + me.z], me.z_dev(d), base)
    for dx, dy in PLANE:
        wires.send(src.at[0, 0:RA], ga.at[me.z * 8 + me.p], me.p_dev(dx, dy), base + 1)


def gather_second(me, wires, ga, gb, base):
    wires.arrived(gb.at[pl.ds(0, 7)], me.z_dev(1), base)
    row = gb.at[pl.ds(me.p * 8, 8)]
    for dx, dy in PLANE:
        wires.send(row, row, me.p_dev(dx, dy), base + 2)
    wires.arrived(ga.at[pl.ds(0, 7)], me.z_dev(1), base + 1)
    row = ga.at[pl.ds(me.z * 8, 8)]
    for d in range(1, Z):
        wires.send(row, row, me.z_dev(d), base + 3)


def gather_last(me, wires, ga, gb, base):
    wires.arrived(gb.at[pl.ds(0, 56)], me.z_dev(1), base + 2)
    wires.arrived(ga.at[pl.ds(0, 56)], me.z_dev(1), base + 3)


def head_lanes(h):
    return pl.ds(pl.multiple_of(h * HD, HD), HD)


def find_reads(mask_ref, owner_ref, table):
    down = lax.broadcasted_iota(jnp.int32, (SLOTS, HD), 0)
    across = lax.broadcasted_iota(jnp.int32, (SLOTS, HD), 1)

    def image(i, reads):
        slot = owner_ref[i]
        hit = down == ((slot // X) % Z) * 8 + (slot // (X * Z)) * X + slot % X
        return tuple(jnp.where(hit, mask_ref[b, i], r) for b, r in enumerate(reads))

    def total(where, what):
        return jnp.sum(jnp.where(where, what, 0), axis=0, keepdims=True)

    zero = jnp.zeros((SLOTS, HD), jnp.int32)
    first, second = lax.fori_loop(0, SLOTS, image, (zero, zero))
    read = jnp.minimum(first + second, 1)
    position = jnp.where(total(down == across, read) > 0, total(down < across, read), READ)
    chosen = jnp.broadcast_to(position, (HD, HD)).T[0:SLOTS] == across
    sub = lax.broadcasted_iota(jnp.int32, (8, HD), 0)
    low = jnp.where(sub == 0, total(chosen, down), total(chosen, first))
    high = jnp.where(sub == 2, total(chosen, second), position)
    turned = lax.rem(down, 8) * 8 + down // 8
    table[...] = jnp.where(sub < 2, low, jnp.where(sub < 4, high, total(chosen, turned)))


def mask_columns(table, dst):
    lane = lax.broadcasted_iota(jnp.int32, (IMG, HD), 1)
    for j in range(READ):
        b0 = jnp.where(table[1, j] > 0, 0.0, -1e30)
        b1 = jnp.where(table[2, j] > 0, 0.0, -1e30)
        bias = jnp.where(lane == 0, b0, jnp.where(lane == 1, b1, 0.0))
        dst[j * IMG : (j + 1) * IMG, HD : 2 * HD] = bias.astype(BF16)


def pick_rows(table, a_ref, b_ref, dst):
    for j in range(READ):
        at = j * IMG
        dst[at : at + RA, 0:HD] = a_ref[table[0, j]]
        dst[at + RA : at + IMG, 0:HD] = b_ref[table[4, j]]


def fold(x, op):
    return op(x.reshape(CHUNK // 8, 8, TOK), axis=0)


def add_rows(acc, k, part):
    acc[k // IMG : (k + CHUNK) // IMG] += part.reshape(CHUNK // IMG, IMG, HD)


def softmax_and_values(q_ref, c_ref, kc, s_ref, p_ref, dv_ref):
    lane = lax.broadcasted_iota(jnp.int32, (TOK, HD), 1)
    row = lax.broadcasted_iota(jnp.int32, (TOK, HD), 0)
    block_of = (lane == row // BLK).astype(BF16)
    chunks = range(0, KEYS, CHUNK)

    def some_heads(i, _):
        heads = [i * TOGETHER + j for j in range(TOGETHER)]
        query = [jnp.concatenate([q_ref[:, head_lanes(h)], block_of], axis=1) for h in heads]
        top = [jnp.full((8, TOK), -jnp.inf, F32) for _ in heads]
        for k in chunks:
            for j in range(TOGETHER):
                s = lax.dot_general(kc[k : k + CHUNK, :], query[j], NT, preferred_element_type=F32)
                top[j] = jnp.maximum(top[j], fold(s, jnp.max))
        top = [jnp.max(t, axis=0, keepdims=True) * SCALE for t in top]
        total = [jnp.zeros((8, TOK), F32) for _ in heads]
        for k in chunks:
            for j in range(TOGETHER):
                s = lax.dot_general(kc[k : k + CHUNK, :], query[j], NT, preferred_element_type=F32)
                e = jnp.exp2(s * SCALE - top[j])
                s_ref[j, k : k + CHUNK, :] = e
                total[j] = total[j] + fold(e, jnp.sum)
        inverse = [1.0 / jnp.sum(t, axis=0, keepdims=True) for t in total]
        cot = jnp.concatenate([c_ref[:, head_lanes(h)] for h in heads], axis=0)
        for k in chunks:
            probs = []
            for j, h in enumerate(heads):
                prob = (s_ref[j, k : k + CHUNK, :] * inverse[j]).astype(BF16)
                p_ref[h, k : k + CHUNK, :] = prob
                probs.append(prob)
            add_rows(dv_ref, k, jnp.dot(jnp.concatenate(probs, axis=1), cot, preferred_element_type=F32))
        return 0

    lax.fori_loop(0, HEADS // TOGETHER, some_heads, 0)


def score_and_keys(q_ref, c_ref, vc, s_ref, p_ref, ds_ref, dk_ref, gate_ref):
    chunks = range(0, KEYS, CHUNK)

    def some_heads(i, _):
        heads = [i * TOGETHER + j for j in range(TOGETHER)]
        cot = [c_ref[:, head_lanes(h)] for h in heads]
        delta = [jnp.zeros((8, TOK), F32) for _ in heads]
        for k in chunks:
            for j, h in enumerate(heads):
                dp = lax.dot_general(vc[k : k + CHUNK, :], cot[j], NT, preferred_element_type=F32)
                s_ref[j, k : k + CHUNK, :] = dp
                delta[j] = delta[j] + fold(dp * p_ref[h, k : k + CHUNK, :].astype(F32), jnp.sum)
        gate_ref[...] += sum(delta)
        delta = [jnp.sum(d, axis=0, keepdims=True) for d in delta]
        query = jnp.concatenate([q_ref[:, head_lanes(h)] for h in heads], axis=0)
        for k in chunks:
            grads = []
            for j, h in enumerate(heads):
                prob = p_ref[h, k : k + CHUNK, :].astype(F32)
                ds = (prob * (s_ref[j, k : k + CHUNK, :] - delta[j])).astype(BF16)
                ds_ref[h, k : k + CHUNK, :] = ds
                grads.append(ds)
            add_rows(dk_ref, k, jnp.dot(jnp.concatenate(grads, axis=1), query, preferred_element_type=F32))
        return 0

    lax.fori_loop(0, HEADS // TOGETHER, some_heads, 0)


def queries_grad(kt, ds_ref, dq_ref, scale):
    def head(h, _):
        t = jnp.dot(kt[...], ds_ref[h], preferred_element_type=F32) * scale
        dq_ref[:, head_lanes(h)] = t.T.astype(BF16)
        return 0

    lax.fori_loop(0, HEADS, head, 0)


def reduce_first(me, wires, table, acc, scale, sa, sb, ra, rb, base):
    def fill_b(p):
        for z in range(Z):
            sb[p * 8 + z] = (acc[table[3, z * 8 + p], RA:IMG] * scale).astype(BF16)

    def fill_a(z):
        for p in range(X * Y):
            sa[z * 8 + p] = (acc[table[3, z * 8 + p], 0:RA] * scale).astype(BF16)

    for dx, dy in PLANE:
        there = me.p_at(dx, dy)
        fill_b(there)
        wires.send(sb.at[pl.ds(there * 8, 8)], rb.at[pl.ds(me.p * 8, 8)], me.p_dev(dx, dy), base)
    for d in range(1, Z):
        there = me.z_at(d)
        fill_a(there)
        wires.send(sa.at[pl.ds(there * 8, 8)], ra.at[pl.ds(me.z * 8, 8)], me.z_dev(d), base + 1)
    fill_b(me.p)
    fill_a(me.z)


def reduce_second(me, wires, sa, sb, ra, rb, ta, tb, ua, ub, base):
    wires.arrived(rb.at[pl.ds(0, 56)], me.z_dev(1), base)
    total = sb[pl.ds(me.p * 8, 8)].astype(F32)
    for dx, dy in PLANE:
        total = total + rb[pl.ds(me.p_at(dx, dy) * 8, 8)].astype(F32)
    tb[...] = total.astype(BF16)
    for d in range(1, Z):
        wires.send(tb.at[me.z_at(d)], ub.at[me.z], me.z_dev(d), base + 2)
    wires.arrived(ra.at[pl.ds(0, 56)], me.z_dev(1), base + 1)
    total = sa[pl.ds(me.z * 8, 8)].astype(F32)
    for d in range(1, Z):
        total = total + ra[pl.ds(me.z_at(d) * 8, 8)].astype(F32)
    ta[...] = total.astype(BF16)
    for dx, dy in PLANE:
        wires.send(ta.at[me.p_at(dx, dy)], ua.at[me.p], me.p_dev(dx, dy), base + 3)


def reduce_last(me, wires, ta, tb, ua, ub, out, base):
    wires.arrived(ub.at[pl.ds(0, 7)], me.z_dev(1), base + 2)
    total = tb[me.z].astype(F32)
    for d in range(1, Z):
        total = total + ub[me.z_at(d)].astype(F32)
    out[0, RA:IMG] = total.astype(BF16)
    wires.arrived(ua.at[pl.ds(0, 7)], me.z_dev(1), base + 3)
    total = ta[me.p].astype(F32)
    for dx, dy in PLANE:
        total = total + ua[me.p_at(dx, dy)].astype(F32)
    out[0, 0:RA] = total.astype(BF16)


def gate_step(wires, own, box, devices, group):
    for i, dev in enumerate(devices):
        wires.send(own, box.at[i], dev, group)

    def finish():
        wires.arrived(box, devices[0], group)
        return own[...] + jnp.sum(box[...], axis=0)

    return finish


def kernel(
    mask_in, owner_in, gate_in, q_in, c_in, k_in, v_in, dq_out, dk_out, dv_out, gate_out,
    mask_ref, owner_ref, gate_ref, table_v, table, q_ref, c_ref, dq_ref,
    ka, kb, va, vb, kc, vc, kt, s_ref, p_ref, ds_ref, dk_ref, dv_ref,
    dka, dkb, dva, dvb, rka, rkb, rva, rvb, tka, tkb, tva, tvb, uka, ukb, uva, uvb,
    gate_rows, gate_own, gate_box, local_sem, send_sem, recv_sem,
):
    me = Place()
    along_z = [me.z_dev(d) for d in range(1, Z)]
    in_plane = [me.p_dev(*d) for d in PLANE]
    along_tp = [me.tp_dev(d) for d in range(1, 8)]
    here_a, here_b = me.z * 8 + me.p, me.p * 8 + me.z
    inputs = [
        pltpu.make_async_copy(src, dst, local_sem.at[i])
        for i, (src, dst) in enumerate(
            (
                (k_in.at[0, 0:RA], ka.at[here_a]),
                (k_in.at[0, RA:IMG], kb.at[here_b]),
                (v_in.at[0, 0:RA], va.at[here_a]),
                (v_in.at[0, RA:IMG], vb.at[here_b]),
                (mask_in, mask_ref),
                (owner_in, owner_ref),
                (gate_in, gate_ref),
                (q_in, q_ref),
                (c_in, c_ref),
            )
        )
    ]
    for one in inputs:
        one.start()
    greet(along_z + in_plane + along_tp)
    wires = Wires(send_sem, recv_sem)
    gather_first(me, wires, k_in, ka, kb, 0)
    gather_first(me, wires, v_in, va, vb, 4)
    for one in inputs:
        one.wait()
    gate = jnp.tanh(jnp.full((1, HD), gate_ref[0], F32))
    find_reads(mask_ref, owner_ref, table_v)
    put = pltpu.make_async_copy(table_v, table, local_sem.at[9])
    put.start()
    dk_ref[...] = jnp.zeros_like(dk_ref)
    dv_ref[...] = jnp.zeros_like(dv_ref)
    gate_rows[...] = jnp.zeros_like(gate_rows)
    put.wait()
    gather_second(me, wires, ka, kb, 0)
    mask_columns(table, kc)
    wires.left(kb.at[pl.ds(0, 56)], me.z_dev(1), 2)
    wires.left(ka.at[pl.ds(0, 56)], me.z_dev(1), 3)
    gather_second(me, wires, va, vb, 4)
    gather_last(me, wires, ka, kb, 0)
    pick_rows(table, ka, kb, kc)
    softmax_and_values(q_ref, c_ref, kc, s_ref, p_ref, dv_ref)
    reduce_first(me, wires, table, dv_ref, gate, dva, dvb, rva, rvb, 8)
    gather_last(me, wires, va, vb, 4)
    pick_rows(table, va, vb, vc)
    score_and_keys(q_ref, c_ref, vc, s_ref, p_ref, ds_ref, dk_ref, gate_rows)
    gate_own[0] = gate_rows[:, 0:HD] + gate_rows[:, HD : 2 * HD]
    step = gate_step(wires, gate_own.at[0], gate_box.at[0], along_z, 16)
    scale = gate * (1.0 / math.sqrt(HD))
    reduce_first(me, wires, table, dk_ref, scale, dka, dkb, rka, rkb, 12)
    kt[...] = kc[:, 0:HD].T
    queries_grad(kt, ds_ref, dq_ref, jnp.concatenate([scale, scale], axis=1))
    back = pltpu.make_async_copy(dq_ref, dq_out, local_sem.at[10])
    back.start()
    reduce_second(me, wires, dva, dvb, rva, rvb, tva, tvb, uva, uvb, 8)
    gate_own[1] = step()
    step = gate_step(wires, gate_own.at[1], gate_box.at[1], in_plane, 17)
    reduce_last(me, wires, tva, tvb, uva, uvb, dv_out, 8)
    gate_own[2] = step()
    step = gate_step(wires, gate_own.at[2], gate_box.at[2], along_tp, 18)
    reduce_second(me, wires, dka, dkb, rka, rkb, tka, tkb, uka, ukb, 12)
    reduce_last(me, wires, tka, tkb, uka, ukb, dk_out, 12)
    gate = jnp.tanh(jnp.full((8, HD), gate_ref[0], F32))
    gate_out[0] = jnp.sum((1.0 - gate * gate) * step()) * (1.0 / math.sqrt(TERMS))
    back.wait()
    wires.drain()


def hand_over(dq, dk, dv, gate, dq_out, dk_out, dv_out, gate_out, dq_here, dk_here, dv_here, sem):
    steps = [(dk, dk_here, dk_out), (dv, dv_here, dv_out)]
    for i in range(4):
        rows = pl.ds(i * 64, 64)
        steps.append((dq.at[rows], dq_here.at[rows], dq_out.at[rows]))
    first = [pltpu.make_async_copy(a, b, sem.at[i]) for i, (a, b, _) in enumerate(steps)]
    second = [pltpu.make_async_copy(b, c, sem.at[6 + i]) for i, (_, b, c) in enumerate(steps)]
    for one in first:
        one.start()
    gate_out[0] = gate[0]
    for one, two in zip(first, second):
        one.wait()
        two.start()
    for two in second:
        two.wait()


def per_device(queries, cotangent, image_keys, image_values, attn_gate, block_mask, image_owner):
    shape = jax.ShapeDtypeStruct
    dma = pltpu.SemaphoreType.DMA
    rows = shape((TOK, HEADS * HD), BF16)
    rows_here = pltpu.VMEM((TOK, HEADS * HD), BF16)
    part_a, part_b = pltpu.VMEM((8, RA, HD), BF16), pltpu.VMEM((8, RB, HD), BF16)
    whole_a, whole_b = pltpu.VMEM((SLOTS, RA, HD), BF16), pltpu.VMEM((SLOTS, RB, HD), BF16)
    grad = shape((1, IMG, HD), BF16)
    anywhere = pl.BlockSpec(memory_space=pltpu.HBM)
    results = pl.pallas_call(
        kernel,
        out_shape=[rows, grad, grad, shape((1,), F32)],
        in_specs=[anywhere] * 7,
        out_specs=[anywhere, VM, VM, SM],
        scratch_shapes=[
            pltpu.SMEM((2, SLOTS), jnp.int32),
            pltpu.SMEM((SLOTS,), jnp.int32),
            pltpu.SMEM((1,), F32),
            pltpu.VMEM((8, HD), jnp.int32),
            pltpu.SMEM((8, HD), jnp.int32),
            rows_here,
            rows_here,
            rows_here,
        ]
        + [whole_a, whole_b] * 2
        + [
            pltpu.VMEM((KEYS, 2 * HD), BF16),
            pltpu.VMEM((KEYS, HD), BF16),
            pltpu.VMEM((HD, KEYS), BF16),
            pltpu.VMEM((TOGETHER, KEYS, TOK), F32),
            pltpu.VMEM((HEADS, KEYS, TOK), BF16),
            pltpu.VMEM((HEADS, KEYS, TOK), BF16),
            pltpu.VMEM((READ + 1, IMG, HD), F32),
            pltpu.VMEM((READ + 1, IMG, HD), F32),
        ]
        + [whole_a, whole_b] * 4
        + [part_a, part_b] * 4
        + [pltpu.VMEM((8, TOK), F32), pltpu.VMEM((3, 8, HD), F32), pltpu.VMEM((3, 7, 8, HD), F32)]
        + [dma((11,)), dma((19,)), dma((19,))],
        compiler_params=pltpu.CompilerParams(
            collective_id=0, has_side_effects=True, vmem_limit_bytes=(64 << 20) - (64 << 10)
        ),
    )(block_mask, image_owner, attn_gate, queries, cotangent, image_keys, image_values)
    return pl.pallas_call(
        hand_over,
        out_shape=[rows, grad, grad, shape((1,), F32)],
        in_specs=[anywhere] * 3 + [SM],
        out_specs=[anywhere] * 3 + [SM],
        scratch_shapes=[rows_here, pltpu.VMEM((1, IMG, HD), BF16), pltpu.VMEM((1, IMG, HD), BF16), dma((12,))],
        compiler_params=pltpu.CompilerParams(vmem_limit_bytes=(64 << 20) - (64 << 10)),
    )(*results)


def solution(mesh):
    specs = (P("ctx", "tp"), P("ctx", "tp"), P("ctx", None, "tp"), P("ctx", None, "tp"), P(), P("ctx", None), P())
    outs = (P("ctx", "tp"), P("ctx", None, "tp"), P("ctx", None, "tp"), P())
    return jax.shard_map(per_device, mesh=mesh, in_specs=specs, out_specs=outs, check_vma=False)
```

time: 77.9 us -> 68.8 us (0.88)
  Pallas kernels: 70.8 us -> 67.3 us
  local copies, waits for them, and re-layouts: 3.21 us -> 0 us
  between operations: 3.1 us -> 1.29 us
    pallas_call x1, Pallas kernels: 70.8 us -> 64.3 us  [per_device(): pl.pallas_call(kernel, out_shape=[rows, grad, grad, shape((1,), F32)], in...]
    unnamed x7 -> x0, local copies, waits for them, and re-layouts: 3.21 us -> none
    pallas_call x0 -> x1, Pallas kernels: none -> 3.01 us  [per_device(): pl.pallas_call(hand_over, out_shape=[rows, grad, grad, shape((1,), F32)],...]
where the time goes in v3:
time: 68.8 us; the launch traced here: 68.6 us
  Pallas kernels  67.3 us (98%)
  between operations  1.29 us (2%)
    pallas_call x1, Pallas kernels, per_device(): pl.pallas_call(kernel, out_shape=[rows, grad, grad, shape((1,), F32)], in...  64.3 us
    pallas_call x1, Pallas kernels, per_device(): pl.pallas_call(hand_over, out_shape=[rows, grad, grad, shape((1,), F32)],...  3.01 us

profile of v3, /device:TPU:1, one launch (start us, length us, event | category | flops | bytes accessed | tf_op | source)
XLA Modules:
  0.0 68.6 jit_solution(8199237834814346549)
XLA Ops:
  1.3 64.3 %shard_map.102 = (bf16[256,1024]{1,0:T(8,128)(2,1)}, bf16[1,64,128]{2,1,0:T(8,128)(2,1)}, bf16[1,64,128]{2,1,0:T(8,128)(2,1)}, f32[1]{0:T(128)}) custom-call(s32[2,64]{1,0:T(2,128)} %mask_in.1, s32[64]{0:T(128)} %owner_in.1, f32[1]{0:T(128)S(6)} %copy.11.gate_in, bf16[256,1024]{1,0:T(8,128)(2,1)} %q_in.1, bf16[256,1024]{1,0:T(8,128)(2,1)} %c_in.1, ...), custom_call_target="tpu_custom_call" | custom-call | tf_op jit(solution)/shard_map/pallas_call | solution.py:413
  65.6 3.0 %shard_map.103 = (bf16[256,1024]{1,0:T(8,128)(2,1)}, bf16[1,64,128]{2,1,0:T(8,128)(2,1)}, bf16[1,64,128]{2,1,0:T(8,128)(2,1)}, f32[1]{0:T(128)}) custom-call(bf16[256,1024]{1,0:T(8,128)(2,1)} %get-tuple-element.8.dq, bf16[1,64,128]{2,1,0:T(8,128)(2,1)} %get-tuple-element.9.dk, bf16[1,64,128]{2,1,0:T(8,128)(2,1)} %get-tuple-element.10.dv, ...), custom_call_target="tpu_custom_call" | custom-call | tf_op jit(solution)/shard_map/pallas_call | solution.py:447

commit v4 on v3

--- a/solution.py
+++ b/solution.py
@@ -26,7 +26,8 @@
 F32 = jnp.float32
 BF16 = jnp.bfloat16
 MESH = pl.DeviceIdType.MESH
-PLANE = [(dx, dy) for dy in range(Y) for dx in range(X) if dx + dy]
+PLANE = ((0, 1), (1, 0), (1, 1), (3, 0), (3, 1), (2, 0), (2, 1))
+LINE = (4, 1, 7, 2, 6, 3, 5)
 VM = pl.BlockSpec(memory_space=pltpu.VMEM)
 SM = pl.BlockSpec(memory_space=pltpu.SMEM)
 
@@ -97,7 +98,7 @@
 
 
 def gather_first(me, wires, src, ga, gb, base):
-    for d in range(1, Z):
+    for d in LINE:
         wires.send(src.at[0, RA:IMG], gb.at[me.p * 8 + me.z], me.z_dev(d), base)
     for dx, dy in PLANE:
         wires.send(src.at[0, 0:RA], ga.at[me.z * 8 + me.p], me.p_dev(dx, dy), base + 1)
@@ -110,7 +111,7 @@
         wires.send(row, row, me.p_dev(dx, dy), base + 2)
     wires.arrived(ga.at[pl.ds(0, 7)], me.z_dev(1), base + 1)
     row = ga.at[pl.ds(me.z * 8, 8)]
-    for d in range(1, Z):
+    for d in LINE:
         wires.send(row, row, me.z_dev(d), base + 3)
 
 
@@ -257,7 +258,7 @@
         there = me.p_at(dx, dy)
         fill_b(there)
         wires.send(sb.at[pl.ds(there * 8, 8)], rb.at[pl.ds(me.p * 8, 8)], me.p_dev(dx, dy), base)
-    for d in range(1, Z):
+    for d in LINE:
         there = me.z_at(d)
         fill_a(there)
         wires.send(sa.at[pl.ds(there * 8, 8)], ra.at[pl.ds(me.z * 8, 8)], me.z_dev(d), base + 1)
@@ -271,11 +272,11 @@
     for dx, dy in PLANE:
         total = total + rb[pl.ds(me.p_at(dx, dy) * 8, 8)].astype(F32)
     tb[...] = total.astype(BF16)
-    for d in range(1, Z):
+    for d in LINE:
         wires.send(tb.at[me.z_at(d)], ub.at[me.z], me.z_dev(d), base + 2)
     wires.arrived(ra.at[pl.ds(0, 56)], me.z_dev(1), base + 1)
     total = sa[pl.ds(me.z * 8, 8)].astype(F32)
-    for d in range(1, Z):
+    for d in LINE:
         total = total + ra[pl.ds(me.z_at(d) * 8, 8)].astype(F32)
     ta[...] = total.astype(BF16)
     for dx, dy in PLANE:
@@ -285,7 +286,7 @@
 def reduce_last(me, wires, ta, tb, ua, ub, out, base):
     wires.arrived(ub.at[pl.ds(0, 7)], me.z_dev(1), base + 2)
     total = tb[me.z].astype(F32)
-    for d in range(1, Z):
+    for d in LINE:
         total = total + ub[me.z_at(d)].astype(F32)
     out[0, RA:IMG] = total.astype(BF16)
     wires.arrived(ua.at[pl.ds(0, 7)], me.z_dev(1), base + 3)
@@ -314,7 +315,7 @@
     gate_rows, gate_own, gate_box, local_sem, send_sem, recv_sem,
 ):
     me = Place()
-    along_z = [me.z_dev(d) for d in range(1, Z)]
+    along_z = [me.z_dev(d) for d in LINE]
     in_plane = [me.p_dev(*d) for d in PLANE]
     along_tp = [me.tp_dev(d) for d in range(1, 8)]
     here_a, here_b = me.z * 8 + me.p, me.p * 8 + me.z

time: 68.8 us -> 69.6 us (1.012)
  Pallas kernels: 67.3 us -> 68.1 us
    pallas_call x1, Pallas kernels: 64.3 us -> 65.1 us  [per_device(): pl.pallas_call(kernel, out_shape=[rows, grad, grad, shape((1,), F32)], in...]
where the time goes in v4:
time: 69.6 us; the launch traced here: 69.4 us
  Pallas kernels  68.1 us (98%)
  between operations  1.29 us (2%)
    pallas_call x1, Pallas kernels, per_device(): pl.pallas_call(kernel, out_shape=[rows, grad, grad, shape((1,), F32)], in...  65.1 us
    pallas_call x1, Pallas kernels, per_device(): pl.pallas_call(hand_over, out_shape=[rows, grad, grad, shape((1,), F32)],...  3.01 us

profile of v4, /device:TPU:1, one launch (start us, length us, event | category | flops | bytes accessed | tf_op | source)
XLA Modules:
  0.0 69.4 jit_solution(5697154848743711971)
XLA Ops:
  1.3 65.1 %shard_map.102 = (bf16[256,1024]{1,0:T(8,128)(2,1)}, bf16[1,64,128]{2,1,0:T(8,128)(2,1)}, bf16[1,64,128]{2,1,0:T(8,128)(2,1)}, f32[1]{0:T(128)}) custom-call(s32[2,64]{1,0:T(2,128)} %mask_in.1, s32[64]{0:T(128)} %owner_in.1, f32[1]{0:T(128)S(6)} %copy.11.gate_in, bf16[256,1024]{1,0:T(8,128)(2,1)} %q_in.1, bf16[256,1024]{1,0:T(8,128)(2,1)} %c_in.1, ...), custom_call_target="tpu_custom_call" | custom-call | tf_op jit(solution)/shard_map/pallas_call | solution.py:414
  66.4 3.0 %shard_map.103 = (bf16[256,1024]{1,0:T(8,128)(2,1)}, bf16[1,64,128]{2,1,0:T(8,128)(2,1)}, bf16[1,64,128]{2,1,0:T(8,128)(2,1)}, f32[1]{0:T(128)}) custom-call(bf16[256,1024]{1,0:T(8,128)(2,1)} %get-tuple-element.8.dq, bf16[1,64,128]{2,1,0:T(8,128)(2,1)} %get-tuple-element.9.dk, bf16[1,64,128]{2,1,0:T(8,128)(2,1)} %get-tuple-element.10.dv, ...), custom_call_target="tpu_custom_call" | custom-call | tf_op jit(solution)/shard_map/pallas_call | solution.py:448

commit v5 on v3

--- a/solution.py
+++ b/solution.py
@@ -96,11 +96,13 @@
                 one.wait_send()
 
 
-def gather_first(me, wires, src, ga, gb, base):
-    for d in range(1, Z):
-        wires.send(src.at[0, RA:IMG], gb.at[me.p * 8 + me.z], me.z_dev(d), base)
-    for dx, dy in PLANE:
-        wires.send(src.at[0, 0:RA], ga.at[me.z * 8 + me.p], me.p_dev(dx, dy), base + 1)
+def gather_first(me, wires, ga, gb, base):
+    for d in range(1, Z):
+        spot = gb.at[me.p * 8 + me.z]
+        wires.send(spot, spot, me.z_dev(d), base)
+    for dx, dy in PLANE:
+        spot = ga.at[me.z * 8 + me.p]
+        wires.send(spot, spot, me.p_dev(dx, dy), base + 1)
 
 
 def gather_second(me, wires, ga, gb, base):
@@ -338,9 +340,11 @@
         one.start()
     greet(along_z + in_plane + along_tp)
     wires = Wires(send_sem, recv_sem)
-    gather_first(me, wires, k_in, ka, kb, 0)
-    gather_first(me, wires, v_in, va, vb, 4)
-    for one in inputs:
+    for one in inputs[:4]:
+        one.wait()
+    gather_first(me, wires, ka, kb, 0)
+    gather_first(me, wires, va, vb, 4)
+    for one in inputs[4:]:
         one.wait()
     gate = jnp.tanh(jnp.full((1, HD), gate_ref[0], F32))
     find_reads(mask_ref, owner_ref, table_v)

time: 68.8 us -> 68.2 us (level)
  no operation moved by 1% of the time
where the time goes in v5:
time: 68.2 us; the launch traced here: 68 us
  Pallas kernels  66.7 us (98%)
  between operations  1.29 us (2%)
    pallas_call x1, Pallas kernels, per_device(): pl.pallas_call(kernel, out_shape=[rows, grad, grad, shape((1,), F32)], in...  63.7 us
    pallas_call x1, Pallas kernels, per_device(): pl.pallas_call(hand_over, out_shape=[rows, grad, grad, shape((1,), F32)],...  3.01 us

profile of v5, /device:TPU:1, one launch (start us, length us, event | category | flops | bytes accessed | tf_op | source)
XLA Modules:
  0.0 68.0 jit_solution(17022517106211457842)
XLA Ops:
  1.3 63.7 %shard_map.102 = (bf16[256,1024]{1,0:T(8,128)(2,1)}, bf16[1,64,128]{2,1,0:T(8,128)(2,1)}, bf16[1,64,128]{2,1,0:T(8,128)(2,1)}, f32[1]{0:T(128)}) custom-call(s32[2,64]{1,0:T(2,128)} %mask_in.1, s32[64]{0:T(128)} %owner_in.1, f32[1]{0:T(128)S(6)} %copy.11.gate_in, bf16[256,1024]{1,0:T(8,128)(2,1)} %q_in.1, bf16[256,1024]{1,0:T(8,128)(2,1)} %c_in.1, ...), custom_call_target="tpu_custom_call" | custom-call | tf_op jit(solution)/shard_map/pallas_call | solution.py:417
  65.0 3.0 %shard_map.103 = (bf16[256,1024]{1,0:T(8,128)(2,1)}, bf16[1,64,128]{2,1,0:T(8,128)(2,1)}, bf16[1,64,128]{2,1,0:T(8,128)(2,1)}, f32[1]{0:T(128)}) custom-call(bf16[256,1024]{1,0:T(8,128)(2,1)} %get-tuple-element.8.dq, bf16[1,64,128]{2,1,0:T(8,128)(2,1)} %get-tuple-element.9.dk, bf16[1,64,128]{2,1,0:T(8,128)(2,1)} %get-tuple-element.10.dv, ...), custom_call_target="tpu_custom_call" | custom-call | tf_op jit(solution)/shard_map/pallas_call | solution.py:451
